TPU v7x, 1024 devices: a whole 8x8x8 slice. The times are simulated.
1024 devices in a mesh: grp: 64 (over x, y), row: 16 (over z, core).
Axes of the slice: x: 8, y: 8, z: 8, core: 2. Of those that a mesh axis runs over, the one named last changes fastest.
Arguments:
- features: bfloat16 [262144, 256], P(('grp', 'row')), may hold values from -6 to 6
- cotangent: bfloat16 [262144, 256], P(('grp', 'row')), may hold values from -6 to 6
- degrees: int32 [262144], P(('grp', 'row')), may hold values from 16 to 64
- tile_cols: int32 [2048, 17], P(('grp', 'row')), may hold values from 0 to 31, as said below
- tile_vals: bfloat16 [2048, 17, 128, 128], P(('grp', 'row')), may hold values from 0 to 1.5, as said below
- w_self: bfloat16 [256, 256], replicated, may hold values from -0.375 to 0.375
- w_neigh: bfloat16 [256, 256], replicated, may hold values from -0.375 to 0.375
Outputs:
- output: bfloat16 [262144, 256], P(('grp', 'row'))
- features_grad: bfloat16 [262144, 256], P(('grp', 'row'))
- w_grads: float32 [2, 256, 256], replicated
Inputs may be any that keep to these rules, and one draw needn't show every extreme that they name: `tile_cols`: in each partition the listed column tiles of row tile R are R + o modulo 32 for one set of 17 distinct offsets o that contains 0 and is closed under negation modulo 32; the set is drawn for each partition. `tile_vals`: the adjacency of each partition is symmetric: the tile listed at (R, C) is the transpose of the tile listed at (C, R), and a tile with R = C is symmetric. Weights lie between 0 and 1.5.
All inputs are finite; a program needn't handle non-finite values.
Results may differ from a plain program's by a relative error of at most 0.014.
Values may be sent and summed in bfloat16 or wider, within the bound.
A program may use at most 32 MiB of HBM per device.

v0:
```python
import jax
import jax.numpy as jnp
from jax import lax
from jax.sharding import PartitionSpec as P


def transpose_dot(left, right):
    return lax.dot_general(
        left, right, (((0,), (0,)), ((), ())), preferred_element_type=jnp.float32
    )


def shards(features, cotangent, degrees, tile_cols, tile_vals, w_self, w_neigh):
    rows, width = features.shape
    tile = tile_vals.shape[2]
    group_rows = rows * lax.axis_size("row")
    count_tiles = group_rows // tile
    row_tiles = rows // tile
    inverse = 1.0 / degrees.astype(jnp.float32)
    group_feats = lax.all_gather(features, "row", axis=0, tiled=True)
    picked = group_feats.reshape(count_tiles, tile, width)[tile_cols]
    summed = jnp.einsum("rsik,rskf->rif", tile_vals, picked, preferred_element_type=jnp.float32)
    aggregate = (summed.reshape(rows, width) * inverse[:, None]).astype(jnp.bfloat16)
    pre_act = jnp.dot(features, w_self, preferred_element_type=jnp.float32) + jnp.dot(
        aggregate, w_neigh, preferred_element_type=jnp.float32
    )
    output = jax.nn.silu(pre_act).astype(jnp.bfloat16)
    sigmoid_z = jax.nn.sigmoid(pre_act)
    grad_pre = (
        cotangent.astype(jnp.float32) * sigmoid_z * (1.0 + pre_act * (1.0 - sigmoid_z))
    ).astype(jnp.bfloat16)
    grad_hidden = (
        jnp.dot(grad_pre, w_neigh.T, preferred_element_type=jnp.float32) * inverse[:, None]
    ).astype(jnp.bfloat16)
    self_grad = jnp.dot(grad_pre, w_self.T, preferred_element_type=jnp.float32)
    terms = jnp.einsum(
        "rsik,rif->rskf",
        tile_vals,
        grad_hidden.reshape(row_tiles, tile, width),
        preferred_element_type=jnp.float32,
    )
    spread = (
        jnp.zeros((count_tiles, tile, width), jnp.float32)
        .at[tile_cols.reshape(-1)]
        .add(terms.reshape(-1, tile, width))
        .reshape(group_rows, width)
    )
    adjoint = lax.psum_scatter(
        spread.astype(jnp.bfloat16), "row", scatter_dimension=0, tiled=True
    ).astype(jnp.float32)
    features_grad = (self_grad + adjoint).astype(jnp.bfloat16)
    scale = float(group_rows * lax.axis_size("grp")) ** (-0.5)
    partial_w = (
        jnp.stack([transpose_dot(features, grad_pre), transpose_dot(aggregate, grad_pre)]) * scale
    )
    w_grads = lax.psum(partial_w, ("grp", "row"))
    return (output, features_grad, w_grads)


def solution(mesh):
    return jax.shard_map(
        shards,
        mesh=mesh,
        in_specs=(
            P(("grp", "row"), None),
            P(("grp", "row"), None),
            P(("grp", "row")),
            P(("grp", "row"), None),
            P(("grp", "row"), None, None, None),
            P(),
            P(),
        ),
        out_specs=(P(("grp", "row"), None), P(("grp", "row"), None), P()),
        check_vma=False,
    )
```

profile of v0, /device:TPU:1, one launch (start us, length us, event | category | flops | bytes accessed | tf_op | source)
XLA Modules:
  0.0 428.0 jit_solution(2497029530366544449)
XLA Ops:
  7.2 0.7 all-gather.2.cloned.1.call-update
  8.0 0.8 reshape.54
  8.7 0.7 compare_select_fusion
  9.5 0.7 convert_divide_fusion
  10.2 1.9 fusion.4
  12.0 58.1 %all-gather.2.cloned.1.call-done = bf16[4096,256]{1,0:T(8,128)(2,1)} async-done(((bf16[256,256]{1,0:T(8,128)(2,1)}), bf16[4096,256]{1,0:T(8,128)(2,1)}) %all-gather.2.cloned.1.call-update) | async-done | bytes 2097168 | tf_op jit(solution)/shard_map/all_gather | solution.py:20
  70.1 2.3 gather_fusion
  72.5 0.5 fusion.6
  73.0 0.1 fusion.2
  73.1 0.3 copy-done.3
  73.5 0.9 multiply_convert_fusion
  74.4 0.2 fusion.1
  74.6 0.2 convolution_bitcast_fusion
  74.9 0.2 convolution_bitcast_fusion.1
  75.1 0.8 maximum_multiply_fusion
  76.0 2.9 fusion.5
  78.9 5.7 %copy.11 = f32[34,128,256]{2,1,0:T(8,128)} copy(f32[34,128,256]{1,2,0:T(8,128)} %bitcast.44) | data formatting | bytes 8912896 | tf_op jit(solution)/shard_map/reshape | solution.py:45
  84.6 2.5 broadcast_in_dim.10
  87.1 14.4 %scatter_fusion = f32[32,128,256]{2,1,0:T(8,128)} fusion(f32[32,128,256]{2,1,0:T(8,128)} %broadcast_in_dim.10, s32[34]{0:T(128)S(1)} %fusion.3, f32[34,128,256]{2,1,0:T(8,128)} %copy.11), kind=kCustom, calls=%fused_computation.1 | custom fusion | flops 1114112 | bytes 13369480 | tf_op jit(solution)/shard_map/scatter-add | solution.py:45
  101.5 3.9 convert_element_type.36
  105.4 254.3 %all-reduce.2.cloned.1.call-done = f32[2,256,256]{1,2,0:T(8,128)} async-done(((f32[2,256,256]{1,2,0:T(8,128)}), f32[2,256,256]{1,2,0:T(8,128)}) %all-reduce.2.cloned.1.call-update) | async-done | bytes 524304 | tf_op jit(solution)/shard_map/psum | solution.py:56
  359.7 2.0 copy.13
  361.8 57.9 %reduce-scatter.2.cloned.1.call-done = bf16[256,256]{1,0:T(8,128)(2,1)} async-done(((bf16[4096,256]{1,0:T(8,128)(2,1)}), bf16[256,256]{1,0:T(8,128)(2,1)}) %reduce-scatter.2.cloned.1.call-update) | async-done | bytes 131088 | tf_op jit(solution)/shard_map/reduce_scatter | solution.py:48
  419.7 1.8 fusion
  (19 shorter events, 0.4 us)
Async XLA Ops:
  7.2 65.3 %copy-start = (bf16[2,17,128,128]{3,2,1,0:T(8,128)(2,1)S(1)}, bf16[2,17,128,128]{3,2,1,0:T(8,128)(2,1)}, u32[]{:S(2)}) copy-start(bf16[2,17,128,128]{3,2,1,0:T(8,128)(2,1)} %param.11) | copy-start | bytes 3342340
  7.2 62.9 %all-gather.2.cloned.1.call-start = ((), (), s32[]{:S(2)}) async-start(), calls=%async_computation.1 | async-start | bytes 2228224 | tf_op jit(solution)/shard_map/all_gather | solution.py:20
  7.9 351.8 %all-reduce.2.cloned.1.call-start = ((), (), s32[]{:S(2)}) async-start(), calls=%async_computation.3 | async-start | bytes 1048576 | tf_op jit(solution)/shard_map/psum | solution.py:56
  72.4 1.0 copy-start.3
  72.4 1.0 copy-start.4
  72.4 1.0 copy-start.5
  72.9 1.9 copy-start.1
  76.0 343.7 %reduce-scatter.2.cloned.1.call-start = ((), (), s32[]{:S(2)}) async-start(), calls=%async_computation.2 | async-start | bytes 2228224 | tf_op jit(solution)/shard_map/reduce_scatter | solution.py:48
  105.4 314.3 %copy-start.2 = (bf16[256,256]{1,0:T(8,128)(2,1)S(1)}, bf16[256,256]{1,0:T(8,128)(2,1)}, u32[]{:S(2)}) copy-start(bf16[256,256]{1,0:T(8,128)(2,1)} %param.12) | copy-start | bytes 393220
Sparse Core Ops, SparseCore 0:
  10.7 59.3 all-gather.1
  76.1 283.6 all-reduce.1
  363.5 56.0 reduce-scatter.1
where the time goes:
time: 430 us; the launch traced here: 428 us
  waiting for transfers between devices  371 us (86%)
  other arithmetic  20.6 us (5%)
  between operations  13.9 us (3%)
  local copies, waits for them, and re-layouts  13.8 us (3%)
  matrix products  8.61 us (2%)
    psum x1, waiting for transfers between devices, shards(): w_grads = lax.psum(partial_w, ('grp', 'row'))  254 us
    all_gather x1, waiting for transfers between devices, shards(): group_feats = lax.all_gather(features, 'row', axis=0, tiled=True)  58.1 us
    reduce_scatter x1, waiting for transfers between devices, shards(): lax.psum_scatter(spread.astype(jnp.bfloat16), 'row', scatter_dimension=0,...  57.9 us
    scatter-add x1, other arithmetic, shards(): spread = jnp.zeros((count_tiles, tile, width), jnp.float32).at[tile_cols....  14.4 us
  transfers between devices with their start and end apart: 3, of which 3 were waited for; matrix products, arithmetic and copies ran while one was open for 8% of the time, Pallas kernels for 0%

commit v1 on v0

v1 whole, which is shorter than its diff:
```python
import functools

import jax
import jax.numpy as jnp
from jax import lax
from jax.experimental import pallas as pl
from jax.experimental.pallas import tpu as pltpu
from jax.sharding import PartitionSpec as P

MESH = pl.DeviceIdType.MESH
BF16 = jnp.bfloat16
F32 = jnp.float32
CORES = 2
CHUNKS = 4


def matmul(left, right):
    return jnp.dot(left, right, preferred_element_type=F32)


def matmul_nt(left, right):
    return lax.dot_general(left, right, (((1,), (1,)), ((), ())), preferred_element_type=F32)


def matmul_tn(left, right):
    return lax.dot_general(left, right, (((0,), (0,)), ((), ())), preferred_element_type=F32)


def layer_kernel(
    side, depth, scale,
    cols, feat, cot, deg, vals, w_self, w_neigh,
    out, fgrad, wgrad,
    feats_all, hidden_all, adj, vals_v, cot_v, deg_v, ws_v, wn_v,
    inv, acc, base, left, gp, out_v, fg_v, wg_v,
    pair_out, pair_in, keep, s1, r1, s2, r2, rz, r4, r5, r6,
    in_sem, out_sem, ring1, ring2, sib1, sib2, ag_send, ar_send, ar_recv,
):
    rows, width = left.shape[1:]
    tile = vals_v.shape[2]
    slots = vals_v.shape[1]
    per_dev = rows // tile
    devs = depth * CORES
    half = depth // 2
    chunk = rows // CHUNKS
    piece = width // side
    tiles2 = s2.shape[1]

    grp, row = lax.axis_index("grp"), lax.axis_index("row")
    gx, gy = lax.div(grp, side), lax.rem(grp, side)
    z, core = lax.div(row, CORES), lax.rem(row, CORES)
    other = 1 - core
    first = (1 - core) * gx + core * gy
    second = (1 - core) * gy + core * gx

    def on_first(p):
        return ((1 - core) * (p * side + gy) + core * (gx * side + p), row)

    def on_second(p):
        return ((1 - core) * (gx * side + p) + core * (p * side + gy), row)

    def on_z(p):
        return (grp, p * CORES + core)

    sibling = (grp, z * CORES + other)

    ins = [
        pltpu.make_async_copy(feat, feats_all.at[row], in_sem.at[0]),
        pltpu.make_async_copy(vals, vals_v, in_sem.at[1]),
        pltpu.make_async_copy(deg, deg_v, in_sem.at[2]),
        pltpu.make_async_copy(w_self, ws_v, in_sem.at[3]),
        pltpu.make_async_copy(w_neigh, wn_v, in_sem.at[4]),
        pltpu.make_async_copy(cot, cot_v, in_sem.at[5]),
    ]
    for copy in ins:
        copy.start()

    barrier = pltpu.get_barrier_semaphore()
    pl.semaphore_signal(barrier, inc=1, device_id=sibling, device_id_type=MESH)

    def greet_z(i, _):
        pl.semaphore_signal(barrier, inc=1, device_id=on_z(lax.rem(z + i, depth)), device_id_type=MESH)
        return 0

    def greet_plane(i, _):
        pl.semaphore_signal(barrier, inc=1, device_id=on_first(lax.rem(first + i, side)), device_id_type=MESH)
        pl.semaphore_signal(barrier, inc=1, device_id=on_second(lax.rem(second + i, side)), device_id_type=MESH)
        return 0

    lax.fori_loop(1, depth, greet_z, 0)
    lax.fori_loop(1, side, greet_plane, 0)
    pl.semaphore_wait(barrier, depth + 2 * (side - 1))

    def owner(q):
        return lax.rem(z - q + depth, depth)

    def ring_copy(buf, recv, way, hop, q, k):
        ref = buf.at[owner(q) * CORES + core, pl.ds(k * chunk, chunk)]
        to = lax.rem(z + 1, depth) if way == 0 else lax.rem(z + depth - 1, depth)
        return pltpu.make_async_remote_copy(
            src_ref=ref, dst_ref=ref, send_sem=ag_send.at[1 if recv is ring2 else 0],
            recv_sem=recv.at[way, hop - 1, k], device_id=on_z(to), device_id_type=MESH)

    def sib_copy(buf, recv, which, q, k):
        ref = buf.at[owner(q) * CORES + core, pl.ds(k * chunk, chunk)]
        return pltpu.make_async_remote_copy(
            src_ref=ref, dst_ref=ref, send_sem=ag_send.at[which],
            recv_sem=recv.at[q], device_id=sibling, device_id_type=MESH)

    def launch(buf, recv, sib, which, k):
        ring_copy(buf, recv, 0, 1, 0, k).start()
        ring_copy(buf, recv, 1, 1, 0, k).start()
        sib_copy(buf, sib, which, 0, k).start()

    def hops(buf, recv, sib, which, hop, k0, k1):
        mid = CHUNKS // 2

        def one(way, k, onward):
            q = hop if way == 0 else depth - hop
            ring_copy(buf, recv, way, hop, q, k).wait_recv()
            if onward:
                ring_copy(buf, recv, way, hop + 1, q, k).start()
            sib_copy(buf, sib, which, q, k).start()

        if hop < half - 1:
            def both(k, _):
                one(0, k, True)
                one(1, k, True)
                return 0
            lax.fori_loop(k0, k1, both, 0)
        elif hop == half - 1:
            for k in range(k0, k1):
                one(0, k, k < mid)
                one(1, k, k >= mid)
        else:
            for k in range(k0, min(k1, mid)):
                one(0, k, False)
                one(1, k + mid, False)

    def sib_wait(buf, sib, which, q):
        block = buf.at[owner(q) * CORES + other]
        pltpu.make_async_remote_copy(
            src_ref=block, dst_ref=block, send_sem=ag_send.at[which],
            recv_sem=sib.at[q], device_id=sibling, device_id_type=MESH).wait_recv()

    def sent(buf, which):
        blocks = buf.at[pl.ds(0, 2 * depth - 1)]
        pltpu.make_async_remote_copy(
            src_ref=blocks, dst_ref=blocks, send_sem=ag_send.at[which],
            recv_sem=sib1.at[0], device_id=sibling, device_id_type=MESH).wait_send()

    def add(buf, q, who):
        b = owner(q) * CORES + who
        acc[...] += matmul(adj[b], buf[b])

    def qs(hop):
        return [0] if hop == 0 else [hop] if hop == half else [hop, depth - hop]

    ins[0].wait()
    for k in range(CHUNKS):
        launch(feats_all, ring1, sib1, 0, k)

    ins[1].wait()

    def build(b, _):
        for i in range(per_dev):
            for j in range(per_dev):
                col = b * per_dev + j
                slot, hit = 0, 0
                for s in range(slots):
                    same = cols[i, s] == col
                    slot = jnp.where(same, s, slot)
                    hit = jnp.where(same, 1, hit)
                adj[b, pl.ds(i * tile, tile), pl.ds(j * tile, tile)] = (
                    vals_v[i, slot] * jnp.float32(hit).astype(BF16))
        return 0

    lax.fori_loop(0, devs, build, 0)

    for copy in ins[2:]:
        copy.wait()
    for i in range(per_dev):
        line = 1.0 / deg_v[pl.ds(i, 1), :].astype(F32)
        square = jnp.transpose(jnp.broadcast_to(line, (tile, tile)))
        for j in range(width // tile):
            inv[pl.ds(i * tile, tile), pl.ds(j * tile, tile)] = square

    left[0] = feats_all[row]
    base[...] = matmul(left[0], ws_v[...])
    acc[...] = matmul(adj[row], left[0])

    for hop in range(1, half + 1):
        hops(feats_all, ring1, sib1, 0, hop, 0, CHUNKS)
        for q in qs(hop - 1):
            sib_wait(feats_all, sib1, 0, q)
            add(feats_all, q, other)
        for q in qs(hop):
            add(feats_all, q, core)
    sib_wait(feats_all, sib1, 0, half)
    add(feats_all, half, other)

    left[1] = (acc[...] * inv[...]).astype(BF16)
    base[...] += matmul(left[1], wn_v[...])
    pre = base[...]
    sig = jax.nn.sigmoid(pre)
    gp[...] = (cot_v[...].astype(F32) * sig * (1.0 + pre * (1.0 - sig))).astype(BF16)
    hidden_all[row] = (matmul_nt(gp[...], wn_v[...]) * inv[...]).astype(BF16)
    for k in range(CHUNKS):
        launch(hidden_all, ring2, sib2, 1, k)

    def spread(src, dst, stage, peer, me, count):
        def send(i, _):
            p = lax.rem(me + i, count)
            pltpu.make_async_remote_copy(
                src_ref=src(p), dst_ref=dst.at[me], send_sem=ar_send.at[stage],
                recv_sem=ar_recv.at[stage], device_id=peer(p), device_id_type=MESH).start()
            return 0
        lax.fori_loop(1, count, send, 0)

    def arrived(dst, stage, count):
        ref = dst.at[pl.ds(0, count - 1)]
        copy = pltpu.make_async_remote_copy(
            src_ref=ref, dst_ref=ref, send_sem=ar_send.at[stage],
            recv_sem=ar_recv.at[stage], device_id=sibling, device_id_type=MESH)
        copy.wait_recv()

    def left_here(dst, stage, count):
        ref = dst.at[pl.ds(0, count - 1)]
        pltpu.make_async_remote_copy(
            src_ref=ref, dst_ref=ref, send_sem=ar_send.at[stage],
            recv_sem=ar_recv.at[stage], device_id=sibling, device_id_type=MESH).wait_send()

    pair = pltpu.make_async_remote_copy(
        src_ref=pair_out, dst_ref=pair_in, send_sem=ar_send.at[0],
        recv_sem=ar_recv.at[0], device_id=sibling, device_id_type=MESH)
    swap = pltpu.make_async_remote_copy(
        src_ref=r5, dst_ref=r6, send_sem=ar_send.at[6],
        recv_sem=ar_recv.at[6], device_id=sibling, device_id_type=MESH)

    def stage0():
        pair_out[...] = matmul_tn(left[other], gp[...]).astype(BF16)
        pair.start()
        keep[...] = matmul_tn(left[core], gp[...])

    def stage1():
        pair.wait_recv()
        for p in range(side):
            part = pl.ds(p * piece, piece)
            s1[p] = (keep[part, :] + pair_in[part, :].astype(F32)).astype(BF16)
        spread(lambda p: s1.at[p], r1, 1, on_first, first, side)
        r1[first] = s1[first]

    def stage2():
        arrived(r1, 1, side)
        total = r1[0].astype(F32)
        for p in range(1, side):
            total += r1[p].astype(F32)
        n = 0
        for i in range(piece // 8):
            for j in range(width // 128):
                s2[n // tiles2, n % tiles2] = total[i * 8:(i + 1) * 8, j * 128:(j + 1) * 128]
                n += 1
        spread(lambda p: s2.at[p], r2, 2, on_second, second, side)
        r2[second] = s2[second]

    def stage3():
        arrived(r2, 2, side)
        total = r2[0]
        for p in range(1, side):
            total += r2[p]
        rz[z] = total
        spread(lambda p: rz.at[z], rz, 3, on_z, z, depth)

    def stage4():
        arrived(rz, 3, depth)
        total = rz[0]
        for p in range(1, depth):
            total += rz[p]
        r4[second] = total * scale
        spread(lambda p: r4.at[second], r4, 4, on_second, second, side)

    def stage5():
        arrived(r4, 4, side)
        n = 0
        for i in range(piece // 8):
            for j in range(width // 128):
                keep[i * 8:(i + 1) * 8, j * 128:(j + 1) * 128] = r4[n // tiles2, n % tiles2]
                n += 1
        r5[first] = keep[0:piece, :].astype(BF16)
        spread(lambda p: r5.at[first], r5, 5, on_first, first, side)

    def stage6():
        arrived(r5, 5, side)
        swap.start()
        for p in range(side):
            wg_v[core, pl.ds(p * piece, piece), :] = r5[p].astype(F32)

    def stage7():
        swap.wait_recv()
        for p in range(side):
            wg_v[other, pl.ds(p * piece, piece), :] = r6[p].astype(F32)

    stage0()
    out_v[...] = (pre * sig).astype(BF16)
    write_out = pltpu.make_async_copy(out_v, out, out_sem.at[0])
    write_out.start()
    acc[...] = matmul_nt(gp[...], ws_v[...])

    step = functools.partial(hops, hidden_all, ring2, sib2, 1)
    stage_after = {(1, 1): stage1, (2, 1): stage2, (2, 3): stage3, (3, 3): stage4, (half, 1): stage5}
    order = [stage1, stage2, stage3, stage4, stage5]
    for hop in range(1, half + 1):
        for k in range(CHUNKS if hop < half else CHUNKS // 2):
            step(hop, k, k + 1)
            if order and stage_after.get((hop, k)) is order[0]:
                order.pop(0)()
        if hop == 1:
            add(hidden_all, 0, core)
        for q in qs(hop - 1):
            sib_wait(hidden_all, sib2, 1, q)
            add(hidden_all, q, other)
        for q in qs(hop):
            add(hidden_all, q, core)
    for stage in order:
        stage()
    sib_wait(hidden_all, sib2, 1, half)
    add(hidden_all, half, other)
    fg_v[...] = acc[...].astype(BF16)
    write_fg = pltpu.make_async_copy(fg_v, fgrad, out_sem.at[1])
    write_fg.start()

    stage6()
    sent(feats_all, 0)
    sent(hidden_all, 1)
    pair.wait_send()
    for buf, stage, count in ((s1, 1, side), (s2, 2, side), (rz, 3, depth), (r4, 4, side), (r5, 5, side)):
        left_here(buf, stage, count)
    stage7()
    write_wg = pltpu.make_async_copy(wg_v, wgrad, out_sem.at[2])
    write_wg.start()
    swap.wait_send()
    write_out.wait()
    write_fg.wait()
    write_wg.wait()


def solution(mesh):
    groups, devs = mesh.shape["grp"], mesh.shape["row"]
    depth = devs // CORES
    side = 1
    while side * side < groups:
        side += 1
    half = depth // 2

    def shards(features, cotangent, degrees, tile_cols, tile_vals, w_self, w_neigh):
        rows, width = features.shape
        row_tiles, slots, tile, _ = tile_vals.shape
        scale = float(rows * devs * groups) ** (-0.5)
        piece = width // side
        tiles2 = piece * width // (8 * 128) // side
        block = (rows, width)
        dma = pltpu.SemaphoreType.DMA
        any_spec = pl.BlockSpec(memory_space=pl.ANY)
        return pl.pallas_call(
            functools.partial(layer_kernel, side, depth, scale),
            out_shape=(
                jax.ShapeDtypeStruct(block, BF16),
                jax.ShapeDtypeStruct(block, BF16),
                jax.ShapeDtypeStruct((2, width, width), F32),
            ),
            in_specs=[pl.BlockSpec(memory_space=pltpu.SMEM)] + [any_spec] * 6,
            out_specs=(any_spec,) * 3,
            scratch_shapes=[
                pltpu.VMEM((devs,) + block, BF16),
                pltpu.VMEM((devs,) + block, BF16),
                pltpu.VMEM((devs, rows, rows), BF16),
                pltpu.VMEM(tile_vals.shape, BF16),
                pltpu.VMEM(block, BF16),
                pltpu.VMEM((row_tiles, tile), jnp.int32),
                pltpu.VMEM((width, width), BF16),
                pltpu.VMEM((width, width), BF16),
                pltpu.VMEM(block, F32),
                pltpu.VMEM(block, F32),
                pltpu.VMEM(block, F32),
                pltpu.VMEM((2,) + block, BF16),
                pltpu.VMEM(block, BF16),
                pltpu.VMEM(block, BF16),
                pltpu.VMEM(block, BF16),
                pltpu.VMEM((2, width, width), F32),
                pltpu.VMEM((width, width), BF16),
                pltpu.VMEM((width, width), BF16),
                pltpu.VMEM((width, width), F32),
                pltpu.VMEM((side, piece, width), BF16),
                pltpu.VMEM((side, piece, width), BF16),
                pltpu.VMEM((side, tiles2, 8, 128), F32),
                pltpu.VMEM((side, tiles2, 8, 128), F32),
                pltpu.VMEM((depth, tiles2, 8, 128), F32),
                pltpu.VMEM((side, tiles2, 8, 128), F32),
                pltpu.VMEM((side, piece, width), BF16),
                pltpu.VMEM((side, piece, width), BF16),
                dma((6,)),
                dma((3,)),
                dma((2, half, CHUNKS)),
                dma((2, half, CHUNKS)),
                dma((depth,)),
                dma((depth,)),
                dma((2,)),
                dma((7,)),
                dma((7,)),
            ],
            compiler_params=pltpu.CompilerParams(
                collective_id=0, has_side_effects=True, vmem_limit_bytes=56 * 1024 * 1024),
        )(
            tile_cols, features, cotangent, degrees.reshape(row_tiles, tile), tile_vals, w_self, w_neigh)

    return jax.shard_map(
        shards,
        mesh=mesh,
        in_specs=(
            P(("grp", "row"), None),
            P(("grp", "row"), None),
            P(("grp", "row")),
            P(("grp", "row"), None),
            P(("grp", "row"), None, None, None),
            P(),
            P(),
        ),
        out_specs=(P(("grp", "row"), None), P(("grp", "row"), None), P()),
        check_vma=False,
    )
```

time: 430 us -> 77.7 us (0.18)
  waiting for transfers between devices: 371 us -> 0 us
  Pallas kernels: 0 us -> 71.8 us
  other arithmetic: 20.6 us -> 0 us
  between operations: 13.9 us -> 0.64 us
  local copies, waits for them, and re-layouts: 13.8 us -> 5 us
  matrix products: 8.61 us -> 0 us
    psum x1 -> x0, waiting for transfers between devices: 254 us -> none  [shards(): w_grads = lax.psum(partial_w, ('grp', 'row'))]
    pallas_call x0 -> x1, Pallas kernels: none -> 71.8 us  [shards(): pl.pallas_call(functools.partial(layer_kernel, side, depth, scale), out_s...]
    all_gather x1 -> x0, waiting for transfers between devices: 58.1 us -> none  [shards(): group_feats = lax.all_gather(features, 'row', axis=0, tiled=True)]
    reduce_scatter x1 -> x0, waiting for transfers between devices: 57.9 us -> none  [shards(): lax.psum_scatter(spread.astype(jnp.bfloat16), 'row', scatter_dimension=0,...]
    scatter-add x1 -> x0, other arithmetic: 14.4 us -> none  [shards(): spread = jnp.zeros((count_tiles, tile, width), jnp.float32).at[tile_cols....]
    dot_general x8 -> x0, matrix products: 8.61 us -> none  [the longest x1 2.89 us: shards(): jnp.einsum('rsik,rif->rskf', tile_vals, grad_hidden.reshape(row_tiles, ti...]
    reshape x2 -> x0, local copies, waits for them, and re-layouts: 6.47 us -> none  [the longest x1 5.71 us: shards(): terms.reshape(-1, tile, width)]
  transfers between devices with their start and end apart: 3 -> 0, of which waited for: 3 -> 0; matrix products, arithmetic and copies ran while one was open for 8% -> 0% of each run, Pallas kernels for 0% -> 0%
where the time goes in v1:
time: 77.7 us; the launch traced here: 77.4 us
  Pallas kernels  71.8 us (92%)
  local copies, waits for them, and re-layouts  5 us (6%)
    pallas_call x1, Pallas kernels, shards(): pl.pallas_call(functools.partial(layer_kernel, side, depth, scale), out_s...  71.8 us
    unnamed x3, local copies, waits for them, and re-layouts  5 us

profile of v1, /device:TPU:1, one launch (start us, length us, event | category | flops | bytes accessed | tf_op | source)
XLA Modules:
  0.0 77.4 jit_solution(9145228567029231102)
XLA Ops:
  0.6 71.8 %shard_map.94 = (bf16[256,256]{1,0:T(8,128)(2,1)}, bf16[256,256]{1,0:T(8,128)(2,1)}, f32[2,256,256]{2,1,0:T(8,128)}) custom-call(s32[2,17]{1,0:T(2,128)} %cols.1, bf16[256,256]{1,0:T(8,128)(2,1)} %feat.1, bf16[256,256]{1,0:T(8,128)(2,1)} %cot.1, s32[2,128]{1,0:T(2,128)} %bitcast.1, bf16[2,17,128,128]{3,2,1,0:T(8,128)(2,1)} %vals.1, bf16[256,256]{1,0:T(8,128)(2,1)} %w_self.1, ...), custom_call_target="tpu_custom_call" | custom-call | tf_op jit(solution)/shard_map/pallas_call | solution.py:363
  72.4 1.6 %copy.13 = bf16[256,256]{1,0:T(8,128)(2,1)} copy(bf16[256,256]{1,0:T(8,128)(2,1)} %get-tuple-element.6) | data formatting | bytes 262144
  74.0 1.6 %copy.14 = bf16[256,256]{1,0:T(8,128)(2,1)} copy(bf16[256,256]{1,0:T(8,128)(2,1)} %get-tuple-element.7) | data formatting | bytes 262144
  75.6 1.9 %copy.15 = f32[2,256,256]{2,1,0:T(8,128)} copy(f32[2,256,256]{2,1,0:T(8,128)} %get-tuple-element.8) | data formatting | bytes 1048576

commit v2 on v1

--- a/solution.py
+++ b/solution.py
@@ -28,12 +28,12 @@
 
 def layer_kernel(
     side, depth, scale,
-    cols, feat, cot, deg, vals, w_self, w_neigh,
+    cols_in, feat, cot, deg, vals, w_self, w_neigh,
     out, fgrad, wgrad,
-    feats_all, hidden_all, adj, vals_v, cot_v, deg_v, ws_v, wn_v,
+    cols, feats_all, hidden_all, adj, vals_v, cot_v, deg_v, ws_v, wn_v,
     inv, acc, base, left, gp, out_v, fg_v, wg_v,
     pair_out, pair_in, keep, s1, r1, s2, r2, rz, r4, r5, r6,
-    in_sem, out_sem, ring1, ring2, sib1, sib2, ag_send, ar_send, ar_recv,
+    in_sem, out_sem, ring1, ring2, sib1, sib2, ag_send, ar_send, ar_recv, relay,
 ):
     rows, width = left.shape[1:]
     tile = vals_v.shape[2]
@@ -41,6 +41,7 @@
     per_dev = rows // tile
     devs = depth * CORES
     half = depth // 2
+    rounds = relay.shape[0]
     chunk = rows // CHUNKS
     piece = width // side
     tiles2 = s2.shape[1]
@@ -70,46 +71,51 @@
         pltpu.make_async_copy(w_self, ws_v, in_sem.at[3]),
         pltpu.make_async_copy(w_neigh, wn_v, in_sem.at[4]),
         pltpu.make_async_copy(cot, cot_v, in_sem.at[5]),
+        pltpu.make_async_copy(cols_in, cols, in_sem.at[6]),
     ]
     for copy in ins:
         copy.start()
 
     barrier = pltpu.get_barrier_semaphore()
-    pl.semaphore_signal(barrier, inc=1, device_id=sibling, device_id_type=MESH)
-
-    def greet_z(i, _):
-        pl.semaphore_signal(barrier, inc=1, device_id=on_z(lax.rem(z + i, depth)), device_id_type=MESH)
-        return 0
-
-    def greet_plane(i, _):
-        pl.semaphore_signal(barrier, inc=1, device_id=on_first(lax.rem(first + i, side)), device_id_type=MESH)
-        pl.semaphore_signal(barrier, inc=1, device_id=on_second(lax.rem(second + i, side)), device_id_type=MESH)
-        return 0
-
-    lax.fori_loop(1, depth, greet_z, 0)
-    lax.fori_loop(1, side, greet_plane, 0)
-    pl.semaphore_wait(barrier, depth + 2 * (side - 1))
+    up, down = lax.rem(z + 1, depth), lax.rem(z + depth - 1, depth)
+    around = [
+        on_first(lax.rem(first + 1, side)), on_first(lax.rem(first + side - 1, side)),
+        on_second(lax.rem(second + 1, side)), on_second(lax.rem(second + side - 1, side)),
+    ]
+    for device in [on_z(up), on_z(down), sibling] + around:
+        pl.semaphore_signal(barrier, inc=1, device_id=device, device_id_type=MESH)
+    pl.semaphore_wait(barrier, 3 + len(around))
+
+    def relay_send(i):
+        for device in around:
+            pl.semaphore_signal(relay.at[i], inc=1, device_id=device, device_id_type=MESH)
+
+    def relay_wait(i):
+        pl.semaphore_wait(relay.at[i], len(around))
 
     def owner(q):
         return lax.rem(z - q + depth, depth)
 
-    def ring_copy(buf, recv, way, hop, q, k):
+    def ring_copy(buf, recv, way, hop, q, k, src=None):
         ref = buf.at[owner(q) * CORES + core, pl.ds(k * chunk, chunk)]
-        to = lax.rem(z + 1, depth) if way == 0 else lax.rem(z + depth - 1, depth)
+        to = up if way == 0 else down
         return pltpu.make_async_remote_copy(
-            src_ref=ref, dst_ref=ref, send_sem=ag_send.at[1 if recv is ring2 else 0],
+            src_ref=ref if src is None else src, dst_ref=ref, send_sem=ag_send.at[1 if recv is ring2 else 0],
             recv_sem=recv.at[way, hop - 1, k], device_id=on_z(to), device_id_type=MESH)
 
-    def sib_copy(buf, recv, which, q, k):
+    def sib_copy(buf, recv, which, q, k, src=None):
         ref = buf.at[owner(q) * CORES + core, pl.ds(k * chunk, chunk)]
         return pltpu.make_async_remote_copy(
-            src_ref=ref, dst_ref=ref, send_sem=ag_send.at[which],
+            src_ref=ref if src is None else src, dst_ref=ref, send_sem=ag_send.at[which],
             recv_sem=recv.at[q], device_id=sibling, device_id_type=MESH)
 
-    def launch(buf, recv, sib, which, k):
-        ring_copy(buf, recv, 0, 1, 0, k).start()
-        ring_copy(buf, recv, 1, 1, 0, k).start()
-        sib_copy(buf, sib, which, 0, k).start()
+    def launch(buf, recv, sib, which, origin):
+        for k in range(CHUNKS):
+            src = origin.at[pl.ds(k * chunk, chunk)]
+            ring_copy(buf, recv, 0, 1, 0, k, src).start()
+            ring_copy(buf, recv, 1, 1, 0, k, src).start()
+        for k in range(CHUNKS):
+            sib_copy(buf, sib, which, 0, k, origin.at[pl.ds(k * chunk, chunk)]).start()
 
     def hops(buf, recv, sib, which, hop, k0, k1):
         mid = CHUNKS // 2
@@ -155,11 +161,11 @@
     def qs(hop):
         return [0] if hop == 0 else [hop] if hop == half else [hop, depth - hop]
 
-    ins[0].wait()
-    for k in range(CHUNKS):
-        launch(feats_all, ring1, sib1, 0, k)
+    launch(feats_all, ring1, sib1, 0, feat)
+    relay_send(0)
 
     ins[1].wait()
+    ins[6].wait()
 
     def build(b, _):
         for i in range(per_dev):
@@ -176,7 +182,7 @@
 
     lax.fori_loop(0, devs, build, 0)
 
-    for copy in ins[2:]:
+    for copy in ins[:1] + ins[2:6]:
         copy.wait()
     for i in range(per_dev):
         line = 1.0 / deg_v[pl.ds(i, 1), :].astype(F32)
@@ -195,6 +201,14 @@
             add(feats_all, q, other)
         for q in qs(hop):
             add(feats_all, q, core)
+        if hop <= rounds:
+            relay_wait(hop - 1)
+            if hop < rounds:
+                relay_send(hop)
+    for i in range(half, rounds):
+        relay_wait(i)
+        if i + 1 < rounds:
+            relay_send(i + 1)
     sib_wait(feats_all, sib1, 0, half)
     add(feats_all, half, other)
 
@@ -203,18 +217,15 @@
     pre = base[...]
     sig = jax.nn.sigmoid(pre)
     gp[...] = (cot_v[...].astype(F32) * sig * (1.0 + pre * (1.0 - sig))).astype(BF16)
-    hidden_all[row] = (matmul_nt(gp[...], wn_v[...]) * inv[...]).astype(BF16)
-    for k in range(CHUNKS):
-        launch(hidden_all, ring2, sib2, 1, k)
+    def far_first(count):
+        return sorted(range(1, count), key=lambda i: (-min(i, count - i), i))
 
     def spread(src, dst, stage, peer, me, count):
-        def send(i, _):
+        for i in far_first(count):
             p = lax.rem(me + i, count)
             pltpu.make_async_remote_copy(
                 src_ref=src(p), dst_ref=dst.at[me], send_sem=ar_send.at[stage],
                 recv_sem=ar_recv.at[stage], device_id=peer(p), device_id_type=MESH).start()
-            return 0
-        lax.fori_loop(1, count, send, 0)
 
     def arrived(dst, stage, count):
         ref = dst.at[pl.ds(0, count - 1)]
@@ -239,15 +250,20 @@
     def stage0():
         pair_out[...] = matmul_tn(left[other], gp[...]).astype(BF16)
         pair.start()
+        hidden_all[row] = (matmul_nt(gp[...], wn_v[...]) * inv[...]).astype(BF16)
+        launch(hidden_all, ring2, sib2, 1, hidden_all.at[row])
         keep[...] = matmul_tn(left[core], gp[...])
 
     def stage1():
         pair.wait_recv()
-        for p in range(side):
-            part = pl.ds(p * piece, piece)
+
+        def ready(p):
+            part = pl.ds(pl.multiple_of(p * piece, piece), piece)
             s1[p] = (keep[part, :] + pair_in[part, :].astype(F32)).astype(BF16)
-        spread(lambda p: s1.at[p], r1, 1, on_first, first, side)
-        r1[first] = s1[first]
+            return s1.at[p]
+
+        spread(ready, r1, 1, on_first, first, side)
+        r1[first] = ready(first)[...]
 
     def stage2():
         arrived(r1, 1, side)
@@ -305,14 +321,11 @@
     write_out.start()
     acc[...] = matmul_nt(gp[...], ws_v[...])
 
-    step = functools.partial(hops, hidden_all, ring2, sib2, 1)
-    stage_after = {(1, 1): stage1, (2, 1): stage2, (2, 3): stage3, (3, 3): stage4, (half, 1): stage5}
-    order = [stage1, stage2, stage3, stage4, stage5]
-    for hop in range(1, half + 1):
-        for k in range(CHUNKS if hop < half else CHUNKS // 2):
-            step(hop, k, k + 1)
-            if order and stage_after.get((hop, k)) is order[0]:
-                order.pop(0)()
+    stage1()
+    for hop, stage in zip(range(1, half + 1), [stage2, stage3, stage4] + [None] * half):
+        hops(hidden_all, ring2, sib2, 1, hop, 0, CHUNKS)
+        if stage is not None and hop < half:
+            stage()
         if hop == 1:
             add(hidden_all, 0, core)
         for q in qs(hop - 1):
@@ -320,7 +333,7 @@
             add(hidden_all, q, other)
         for q in qs(hop):
             add(hidden_all, q, core)
-    for stage in order:
+    for stage in [stage2, stage3, stage4][half - 1:]:
         stage()
     sib_wait(hidden_all, sib2, 1, half)
     add(hidden_all, half, other)
@@ -328,6 +341,7 @@
     write_fg = pltpu.make_async_copy(fg_v, fgrad, out_sem.at[1])
     write_fg.start()
 
+    stage5()
     stage6()
     sent(feats_all, 0)
     sent(hidden_all, 1)
@@ -343,6 +357,17 @@
     write_wg.wait()
 
 
+def deliver(out_in, fgrad_in, wgrad_in, out, fgrad, wgrad, sem):
+    copies = [
+        pltpu.make_async_copy(src, dst, sem.at[i])
+        for i, (src, dst) in enumerate([(out_in, out), (fgrad_in, fgrad), (wgrad_in, wgrad)])
+    ]
+    for copy in copies:
+        copy.start()
+    for copy in copies:
+        copy.wait()
+
+
 def solution(mesh):
     groups, devs = mesh.shape["grp"], mesh.shape["row"]
     depth = devs // CORES
@@ -360,16 +385,18 @@
         block = (rows, width)
         dma = pltpu.SemaphoreType.DMA
         any_spec = pl.BlockSpec(memory_space=pl.ANY)
-        return pl.pallas_call(
+        hbm = pl.BlockSpec(memory_space=pltpu.HBM)
+        results = pl.pallas_call(
             functools.partial(layer_kernel, side, depth, scale),
             out_shape=(
                 jax.ShapeDtypeStruct(block, BF16),
                 jax.ShapeDtypeStruct(block, BF16),
                 jax.ShapeDtypeStruct((2, width, width), F32),
             ),
-            in_specs=[pl.BlockSpec(memory_space=pltpu.SMEM)] + [any_spec] * 6,
-            out_specs=(any_spec,) * 3,
+            in_specs=[hbm] * 7,
+            out_specs=(pl.BlockSpec(memory_space=pltpu.VMEM),) * 3,
             scratch_shapes=[
+                pltpu.SMEM(tile_cols.shape, jnp.int32),
                 pltpu.VMEM((devs,) + block, BF16),
                 pltpu.VMEM((devs,) + block, BF16),
                 pltpu.VMEM((devs, rows, rows), BF16),
@@ -397,7 +424,7 @@
                 pltpu.VMEM((side, tiles2, 8, 128), F32),
                 pltpu.VMEM((side, piece, width), BF16),
                 pltpu.VMEM((side, piece, width), BF16),
-                dma((6,)),
+                dma((7,)),
                 dma((3,)),
                 dma((2, half, CHUNKS)),
                 dma((2, half, CHUNKS)),
@@ -406,11 +433,20 @@
                 dma((2,)),
                 dma((7,)),
                 dma((7,)),
+                pltpu.SemaphoreType.REGULAR((max(1, side // 2 - 1),)),
             ],
             compiler_params=pltpu.CompilerParams(
                 collective_id=0, has_side_effects=True, vmem_limit_bytes=56 * 1024 * 1024),
         )(
             tile_cols, features, cotangent, degrees.reshape(row_tiles, tile), tile_vals, w_self, w_neigh)
+        return pl.pallas_call(
+            deliver,
+            out_shape=[jax.ShapeDtypeStruct(r.shape, r.dtype) for r in results],
+            in_specs=[pl.BlockSpec(memory_space=pltpu.VMEM)] * 3,
+            out_specs=[hbm] * 3,
+            scratch_shapes=[dma((3,))],
+            compiler_params=pltpu.CompilerParams(vmem_limit_bytes=56 * 1024 * 1024),
+        )(*results)
 
     return jax.shard_map(
         shards,

time: 77.7 us -> 69.3 us (0.89)
  local copies, waits for them, and re-layouts: 5 us -> 0 us
  Pallas kernels: 71.8 us -> 68.5 us
    pallas_call x1, Pallas kernels: 71.8 us -> 66.4 us  [shards(): pl.pallas_call(functools.partial(layer_kernel, side, depth, scale), out_s...]
    unnamed x3 -> x0, local copies, waits for them, and re-layouts: 5 us -> none
    pallas_call x0 -> x1, Pallas kernels: none -> 2.08 us  [shards(): pl.pallas_call(deliver, out_shape=[jax.ShapeDtypeStruct(r.shape, r.dtype)...]
where the time goes in v2:
time: 69.3 us; the launch traced here: 69.1 us
  Pallas kernels  68.5 us (99%)
    pallas_call x1, Pallas kernels, shards(): pl.pallas_call(functools.partial(layer_kernel, side, depth, scale), out_s...  66.4 us
    pallas_call x1, Pallas kernels, shards(): pl.pallas_call(deliver, out_shape=[jax.ShapeDtypeStruct(r.shape, r.dtype)...  2.08 us

profile of v2, /device:TPU:1, one launch (start us, length us, event | category | flops | bytes accessed | tf_op | source)
XLA Modules:
  0.0 69.1 jit_solution(14350037309806999549)
XLA Ops:
  0.6 66.4 %shard_map.94 = (bf16[256,256]{1,0:T(8,128)(2,1)}, bf16[256,256]{1,0:T(8,128)(2,1)}, f32[2,256,256]{2,1,0:T(8,128)}) custom-call(s32[2,17]{1,0:T(2,128)} %cols_in.1, bf16[256,256]{1,0:T(8,128)(2,1)} %feat.1, bf16[256,256]{1,0:T(8,128)(2,1)} %cot.1, s32[2,128]{1,0:T(2,128)} %bitcast.1, bf16[2,17,128,128]{3,2,1,0:T(8,128)(2,1)} %vals.1, ...), custom_call_target="tpu_custom_call" | custom-call | tf_op jit(solution)/shard_map/pallas_call | solution.py:389
  67.0 2.1 %shard_map.95 = (bf16[256,256]{1,0:T(8,128)(2,1)}, bf16[256,256]{1,0:T(8,128)(2,1)}, f32[2,256,256]{2,1,0:T(8,128)}) custom-call(bf16[256,256]{1,0:T(8,128)(2,1)} %get-tuple-element.6.out_in, bf16[256,256]{1,0:T(8,128)(2,1)} %get-tuple-element.7.fgrad_in, f32[2,256,256]{2,1,0:T(8,128)} %get-tuple-element.8.wgrad_in), custom_call_target="tpu_custom_call" | custom-call | tf_op jit(solution)/shard_map/pallas_call | solution.py:442

commit v3 on v2

v3 whole, which is shorter than its diff:
```python
import functools

import jax
import jax.numpy as jnp
from jax import lax
from jax.experimental import pallas as pl
from jax.experimental.pallas import tpu as pltpu
from jax.sharding import PartitionSpec as P

MESH = pl.DeviceIdType.MESH
BF16 = jnp.bfloat16
F32 = jnp.float32
CORES = 2
CHUNKS = 4


def matmul(left, right):
    return jnp.dot(left, right, preferred_element_type=F32)


def matmul_nt(left, right):
    return lax.dot_general(left, right, (((1,), (1,)), ((), ())), preferred_element_type=F32)


def matmul_tn(left, right):
    return lax.dot_general(left, right, (((0,), (0,)), ((), ())), preferred_element_type=F32)


def layer_kernel(
    side, depth, scale,
    cols_in, feat, cot, deg, vals, w_self, w_neigh,
    out, fgrad, wgrad,
    cols, places_v, places, feats_all, hidden_all, adj, vals_v, cot_v, deg_v, ws_v, wn_v,
    inv, acc, base, left, gp, out_v, fg_v,
    pair_out, pair_in, keep, s1, r1, r2, r3, r5,
    in_sem, out_sem, ring, near, sib, ag_send, ar_send, ar_recv, relay,
):
    rows, width = left.shape[1:]
    tile = vals_v.shape[2]
    slots = vals_v.shape[1]
    per_dev = rows // tile
    devs = depth * CORES
    half = depth // 2
    rounds = relay.shape[0]
    chunk = rows // CHUNKS
    piece = width // side

    grp, row = lax.axis_index("grp"), lax.axis_index("row")
    gx, gy = lax.div(grp, side), lax.rem(grp, side)
    z, core = lax.div(row, CORES), lax.rem(row, CORES)
    other = 1 - core
    first = (1 - core) * gx + core * gy
    second = (1 - core) * gy + core * gx

    def on_first(p):
        return ((1 - core) * (p * side + gy) + core * (gx * side + p), row)

    def on_second(p):
        return ((1 - core) * (gx * side + p) + core * (p * side + gy), row)

    def on_z(p):
        return (grp, p * CORES + core)

    sibling = (grp, z * CORES + other)

    ins = [
        pltpu.make_async_copy(feat, feats_all.at[row], in_sem.at[0]),
        pltpu.make_async_copy(vals, vals_v, in_sem.at[1]),
        pltpu.make_async_copy(deg, deg_v, in_sem.at[2]),
        pltpu.make_async_copy(w_self, ws_v, in_sem.at[3]),
        pltpu.make_async_copy(w_neigh, wn_v, in_sem.at[4]),
        pltpu.make_async_copy(cot, cot_v, in_sem.at[5]),
        pltpu.make_async_copy(cols_in, cols, in_sem.at[6]),
    ]
    for copy in ins:
        copy.start()

    barrier = pltpu.get_barrier_semaphore()
    up, down = lax.rem(z + 1, depth), lax.rem(z + depth - 1, depth)
    around = [
        on_first(lax.rem(first + 1, side)), on_first(lax.rem(first + side - 1, side)),
        on_second(lax.rem(second + 1, side)), on_second(lax.rem(second + side - 1, side)),
    ]
    for device in [on_z(up), on_z(down), sibling] + around:
        pl.semaphore_signal(barrier, inc=1, device_id=device, device_id_type=MESH)
    pl.semaphore_wait(barrier, 3 + len(around))

    def relay_send(i):
        for device in around:
            pl.semaphore_signal(relay.at[i], inc=1, device_id=device, device_id_type=MESH)

    def relay_wait(i):
        pl.semaphore_wait(relay.at[i], len(around))

    onward = on_z(core * down + other * up)

    def chip(hop):
        return lax.rem(z + (2 * core - 1) * hop + depth, depth)

    def part(buf, hop, own, k):
        who = core if own else other
        return buf.at[chip(hop) * CORES + who, pl.ds(k * chunk, chunk)]

    def ring_copy(buf, which, hop, own, k, src=None):
        ref = part(buf, hop, own, k)
        return pltpu.make_async_remote_copy(
            src_ref=ref if src is None else src, dst_ref=ref, send_sem=ag_send.at[which],
            recv_sem=ring.at[which, 0 if own else 1, hop, k], device_id=onward, device_id_type=MESH)

    def ring_wait(buf, which, hop, own, k):
        ref = part(buf, hop, own, k)
        pltpu.make_async_remote_copy(
            src_ref=ref, dst_ref=ref, send_sem=ag_send.at[which],
            recv_sem=ring.at[which, 0 if own else 1, hop - 1, k],
            device_id=onward, device_id_type=MESH).wait_recv()

    def sib_copy(ref, which, sem, src=None):
        return pltpu.make_async_remote_copy(
            src_ref=ref if src is None else src, dst_ref=ref, send_sem=ag_send.at[which],
            recv_sem=sem, device_id=sibling, device_id_type=MESH)

    def launch_own(buf, which, origin):
        for k in range(CHUNKS):
            src = origin.at[pl.ds(k * chunk, chunk)]
            sib_copy(part(buf, 0, True, k), which, near.at[which, k], src).start()
            ring_copy(buf, which, 0, True, k, src).start()

    def launch_other(buf, which):
        def one(k, _):
            sib_copy(part(buf, 0, False, k), which, near.at[which, k]).wait_recv()
            ring_copy(buf, which, 0, False, k).start()
            return 0
        lax.fori_loop(0, CHUNKS, one, 0)

    def hop_in(buf, which, hop):
        for own in (True, False)[:2 if hop < half else 1]:
            def one(k, _):
                ring_wait(buf, which, hop, own, k)
                if hop < half - 1 or (hop == half - 1 and own):
                    ring_copy(buf, which, hop, own, k).start()
                sib_copy(part(buf, hop, own, k), which, sib.at[which, hop - 1, 0 if own else 1]).start()
                return 0
            lax.fori_loop(0, CHUNKS, one, 0)

    def sib_in(buf, which, hop):
        for i in range(2 if hop < half else 1):
            block = buf.at[0]
            sib_copy(block, which, sib.at[which, hop - 1, i]).wait_recv()

    def sent(buf, which):
        blocks = buf.at[pl.ds(0, 2 * depth - 1)]
        sib_copy(blocks, which, near.at[which, 0]).wait_send()

    def add(buf, hop):
        at = chip(hop)
        acc[...] += matmul(adj[at], buf[pl.ds(CORES * at, CORES)].reshape(CORES * rows, width))

    launch_own(feats_all, 0, feat)
    relay_send(0)
    launch_other(feats_all, 0)

    ins[6].wait()
    lane = lax.broadcasted_iota(jnp.int32, (per_dev, 128), 1)
    place, listed = jnp.zeros_like(lane), jnp.zeros_like(lane)
    for s in range(slots):
        same = cols[:, s:s + 1] == lane
        place = jnp.where(same, s, place)
        listed = jnp.where(same, 1, listed)
    places_v[0:per_dev, :] = place
    places_v[per_dev:2 * per_dev, :] = listed
    to_scalar = pltpu.make_async_copy(places_v, places, in_sem.at[7])
    to_scalar.start()
    ins[1].wait()
    to_scalar.wait()

    def build(hop):
        at = chip(hop)
        for i in range(per_dev):
            for j in range(CORES * per_dev):
                col = at * (CORES * per_dev) + j
                listed = places[per_dev + i, col]
                adj[at, pl.ds(i * tile, tile), pl.ds(j * tile, tile)] = (
                    vals_v[i, places[i, col]] * jnp.float32(listed).astype(BF16))

    build(0)
    for copy in ins[:1] + ins[2:6]:
        copy.wait()
    for i in range(per_dev):
        line = 1.0 / deg_v[pl.ds(i, 1), :].astype(F32)
        square = jnp.transpose(jnp.broadcast_to(line, (tile, tile)))
        for j in range(width // tile):
            inv[pl.ds(i * tile, tile), pl.ds(j * tile, tile)] = square

    left[0] = feats_all[row]
    base[...] = matmul(left[0], ws_v[...])
    acc[...] = jnp.zeros_like(acc)
    add(feats_all, 0)
    for hop in range(1, half + 1):
        hop_in(feats_all, 0, hop)
        build(hop)
        if hop < half:
            build(-hop)
            add(feats_all, hop)
        if 1 < hop <= rounds + 1:
            relay_wait(hop - 2)
            if hop <= rounds:
                relay_send(hop - 1)
    for hop in range(1, half + 1):
        sib_in(feats_all, 0, hop)
        add(feats_all, -hop)
    for i in range(half - 1, rounds):
        relay_wait(i)
        if i + 1 < rounds:
            relay_send(i + 1)

    left[1] = (acc[...] * inv[...]).astype(BF16)
    base[...] += matmul(left[1], wn_v[...])
    pre = base[...]
    sig = jax.nn.sigmoid(pre)
    gp[...] = (cot_v[...].astype(F32) * sig * (1.0 + pre * (1.0 - sig))).astype(BF16)
    def far_first(count):
        return sorted(range(1, count), key=lambda i: (-min(i, count - i), i))

    def spread(src, dst, stage, peer, me, count):
        for i in far_first(count):
            p = lax.rem(me + i, count)
            pltpu.make_async_remote_copy(
                src_ref=src(p), dst_ref=dst.at[me], send_sem=ar_send.at[stage],
                recv_sem=ar_recv.at[stage], device_id=peer(p), device_id_type=MESH).start()

    def arrived(dst, stage, count):
        ref = dst.at[pl.ds(0, count - 1)]
        copy = pltpu.make_async_remote_copy(
            src_ref=ref, dst_ref=ref, send_sem=ar_send.at[stage],
            recv_sem=ar_recv.at[stage], device_id=sibling, device_id_type=MESH)
        copy.wait_recv()

    def left_here(dst, stage, count):
        ref = dst.at[pl.ds(0, count - 1)]
        pltpu.make_async_remote_copy(
            src_ref=ref, dst_ref=ref, send_sem=ar_send.at[stage],
            recv_sem=ar_recv.at[stage], device_id=sibling, device_id_type=MESH).wait_send()

    pair = pltpu.make_async_remote_copy(
        src_ref=pair_out, dst_ref=pair_in, send_sem=ar_send.at[0],
        recv_sem=ar_recv.at[0], device_id=sibling, device_id_type=MESH)
    swap = pltpu.make_async_remote_copy(
        src_ref=r5, dst_ref=wgrad.at[core], send_sem=ar_send.at[6],
        recv_sem=ar_recv.at[6], device_id=sibling, device_id_type=MESH)

    write_wg = pltpu.make_async_copy(r5, wgrad.at[core], out_sem.at[2])

    def stage0():
        pair_out[...] = matmul_tn(left[other], gp[...]).astype(BF16)
        pair.start()
        hidden_all[row] = (matmul_nt(gp[...], wn_v[...]) * inv[...]).astype(BF16)
        launch_own(hidden_all, 1, hidden_all.at[row])
        keep[...] = matmul_tn(left[core], gp[...])

    def stage1():
        pair.wait_recv()

        def ready(p):
            part = pl.ds(pl.multiple_of(p * piece, piece), piece)
            s1[p] = (keep[part, :] + pair_in[part, :].astype(F32)).astype(BF16)
            return s1.at[p]

        spread(ready, r1, 1, on_first, first, side)
        r1[first] = ready(first)[...]

    z_early = core if side == depth else 0

    def on_cross(by_z, p):
        across, along = on_second(p), on_z(p)
        return tuple(by_z * a + (1 - by_z) * b for a, b in zip(along, across))

    def total(ref, count):
        value = ref[0].astype(F32)
        for p in range(1, count):
            value += ref[p].astype(F32)
        return value

    def cross(by_z, dst, stage, count, value):
        me = by_z * z + (1 - by_z) * second
        dst[me] = value.astype(BF16)
        spread(lambda p: dst.at[me], dst, stage, functools.partial(on_cross, by_z), me, count)

    def stage2():
        arrived(r1, 1, side)
        cross(z_early, r2, 2, side, total(r1, side))

    def stage3():
        arrived(r2, 2, side)
        cross(1 - z_early, r3, 3, depth, total(r2, side))

    def stage5():
        arrived(r3, 3, depth)
        r5[first] = (total(r3, depth) * scale).astype(BF16)
        spread(lambda p: r5.at[first], r5, 5, on_first, first, side)

    def stage6():
        arrived(r5, 5, side)
        swap.start()
        write_wg.start()

    stage0()
    stage1()
    launch_other(hidden_all, 1)
    out_v[...] = (pre * sig).astype(BF16)
    write_out = pltpu.make_async_copy(out_v, out, out_sem.at[0])
    write_out.start()
    acc[...] = matmul_nt(gp[...], ws_v[...])
    add(hidden_all, 0)
    stages = [stage2, stage3, stage5]
    for hop in range(1, half + 1):
        hop_in(hidden_all, 1, hop)
        if stages:
            stages.pop(0)()
        if hop < half:
            add(hidden_all, hop)
    for stage in stages:
        stage()
    for hop in range(1, half + 1):
        sib_in(hidden_all, 1, hop)
        add(hidden_all, -hop)
    fg_v[...] = acc[...].astype(BF16)
    write_fg = pltpu.make_async_copy(fg_v, fgrad, out_sem.at[1])
    write_fg.start()

    stage6()
    sent(feats_all, 0)
    sent(hidden_all, 1)
    pair.wait_send()
    for buf, stage, count in ((s1, 1, side), (r2, 2, side), (r3, 3, depth), (r5, 5, side)):
        left_here(buf, stage, count)
    swap.wait()
    write_out.wait()
    write_fg.wait()
    write_wg.wait()


def deliver(out_in, fgrad_in, wgrad_in, out, fgrad, wgrad):
    out[...] = out_in[...]
    fgrad[...] = fgrad_in[...]
    wgrad[...] = wgrad_in[...].astype(F32).reshape(wgrad.shape)


def solution(mesh):
    groups, devs = mesh.shape["grp"], mesh.shape["row"]
    depth = devs // CORES
    side = 1
    while side * side < groups:
        side += 1
    half = depth // 2

    def shards(features, cotangent, degrees, tile_cols, tile_vals, w_self, w_neigh):
        rows, width = features.shape
        row_tiles, slots, tile, _ = tile_vals.shape
        scale = float(rows * devs * groups) ** (-0.5)
        piece = width // side
        block = (rows, width)
        dma = pltpu.SemaphoreType.DMA
        any_spec = pl.BlockSpec(memory_space=pl.ANY)
        hbm = pl.BlockSpec(memory_space=pltpu.HBM)
        results = pl.pallas_call(
            functools.partial(layer_kernel, side, depth, scale),
            out_shape=(
                jax.ShapeDtypeStruct(block, BF16),
                jax.ShapeDtypeStruct(block, BF16),
                jax.ShapeDtypeStruct((2, side, piece, width), BF16),
            ),
            in_specs=[hbm] * 7,
            out_specs=(any_spec,) * 3,
            scratch_shapes=[
                pltpu.VMEM(tile_cols.shape, jnp.int32),
                pltpu.VMEM((2 * row_tiles, 128), jnp.int32),
                pltpu.SMEM((2 * row_tiles, 128), jnp.int32),
                pltpu.VMEM((devs,) + block, BF16),
                pltpu.VMEM((devs,) + block, BF16),
                pltpu.VMEM((depth, rows, CORES * rows), BF16),
                pltpu.VMEM(tile_vals.shape, BF16),
                pltpu.VMEM(block, BF16),
                pltpu.VMEM((row_tiles, tile), jnp.int32),
                pltpu.VMEM((width, width), BF16),
                pltpu.VMEM((width, width), BF16),
                pltpu.VMEM(block, F32),
                pltpu.VMEM(block, F32),
                pltpu.VMEM(block, F32),
                pltpu.VMEM((2,) + block, BF16),
                pltpu.VMEM(block, BF16),
                pltpu.VMEM(block, BF16),
                pltpu.VMEM(block, BF16),
                pltpu.VMEM((width, width), BF16),
                pltpu.VMEM((width, width), BF16),
                pltpu.VMEM((width, width), F32),
                pltpu.VMEM((side, piece, width), BF16),
                pltpu.VMEM((side, piece, width), BF16),
                pltpu.VMEM((side, piece, width), BF16),
                pltpu.VMEM((depth, piece, width), BF16),
                pltpu.VMEM((side, piece, width), BF16),
                dma((8,)),
                dma((3,)),
                dma((2, 2, half, CHUNKS)),
                dma((2, CHUNKS)),
                dma((2, half, 2)),
                dma((2,)),
                dma((7,)),
                dma((7,)),
                pltpu.SemaphoreType.REGULAR((max(1, side // 2 - 1),)),
            ],
            compiler_params=pltpu.CompilerParams(
                collective_id=0, has_side_effects=True, vmem_limit_bytes=56 * 1024 * 1024),
        )(
            tile_cols, features, cotangent, degrees.reshape(row_tiles, tile), tile_vals, w_self, w_neigh)
        whole = pl.BlockSpec(memory_space=pltpu.VMEM)
        return pl.pallas_call(
            deliver,
            out_shape=(
                jax.ShapeDtypeStruct(block, BF16),
                jax.ShapeDtypeStruct(block, BF16),
                jax.ShapeDtypeStruct((2, width, width), F32),
            ),
            in_specs=[whole] * 3,
            out_specs=(whole,) * 3,
            compiler_params=pltpu.CompilerParams(vmem_limit_bytes=56 * 1024 * 1024),
        )(*results)

    return jax.shard_map(
        shards,
        mesh=mesh,
        in_specs=(
            P(("grp", "row"), None),
            P(("grp", "row"), None),
            P(("grp", "row")),
            P(("grp", "row"), None),
            P(("grp", "row"), None, None, None),
            P(),
            P(),
        ),
        out_specs=(P(("grp", "row"), None), P(("grp", "row"), None), P()),
        check_vma=False,
    )
```

time: 69.3 us -> 63.1 us (0.911)
  Pallas kernels: 68.5 us -> 62.3 us
    pallas_call x1, Pallas kernels: 66.4 us -> 60.3 us  [shards(): pl.pallas_call(functools.partial(layer_kernel, side, depth, scale), out_s...]
where the time goes in v3:
time: 63.1 us; the launch traced here: 62.9 us
  Pallas kernels  62.3 us (99%)
  between operations  0.64 us (1%)
    pallas_call x1, Pallas kernels, shards(): pl.pallas_call(functools.partial(layer_kernel, side, depth, scale), out_s...  60.3 us
    pallas_call x1, Pallas kernels, shards(): pl.pallas_call(deliver, out_shape=(jax.ShapeDtypeStruct(block, BF16), jax...  1.97 us

profile of v3, /device:TPU:1, one launch (start us, length us, event | category | flops | bytes accessed | tf_op | source)
XLA Modules:
  0.0 62.9 jit_solution(6112967306170259938)
XLA Ops:
  0.6 60.3 %shard_map.94 = (bf16[256,256]{1,0:T(8,128)(2,1)}, bf16[256,256]{1,0:T(8,128)(2,1)}, bf16[2,8,32,256]{3,2,1,0:T(8,128)(2,1)}) custom-call(s32[2,17]{1,0:T(2,128)} %cols_in.1, bf16[256,256]{1,0:T(8,128)(2,1)} %feat.1, bf16[256,256]{1,0:T(8,128)(2,1)} %cot.1, s32[2,128]{1,0:T(2,128)} %bitcast.1, bf16[2,17,128,128]{3,2,1,0:T(8,128)(2,1)} %vals.1, ...), custom_call_target="tpu_custom_call" | custom-call | tf_op jit(solution)/shard_map/pallas_call | solution.py:365
  61.0 2.0 %shard_map.95 = (bf16[256,256]{1,0:T(8,128)(2,1)}, bf16[256,256]{1,0:T(8,128)(2,1)}, f32[2,256,256]{2,1,0:T(8,128)}) custom-call(bf16[256,256]{1,0:T(8,128)(2,1)} %get-tuple-element.6.out_in, bf16[256,256]{1,0:T(8,128)(2,1)} %get-tuple-element.7.fgrad_in, bf16[2,8,32,256]{3,2,1,0:T(8,128)(2,1)} %get-tuple-element.8.wgrad_in), custom_call_target="tpu_custom_call" | custom-call | tf_op jit(solution)/shard_map/pallas_call | solution.py:416

commit v4 on v3

--- a/solution.py
+++ b/solution.py
@@ -20,10 +20,6 @@
 
 def matmul_nt(left, right):
     return lax.dot_general(left, right, (((1,), (1,)), ((), ())), preferred_element_type=F32)
-
-
-def matmul_tn(left, right):
-    return lax.dot_general(left, right, (((0,), (0,)), ((), ())), preferred_element_type=F32)
 
 
 def layer_kernel(
@@ -35,7 +31,7 @@
     pair_out, pair_in, keep, s1, r1, r2, r3, r5,
     in_sem, out_sem, ring, near, sib, ag_send, ar_send, ar_recv, relay,
 ):
-    rows, width = left.shape[1:]
+    rows, width = gp.shape
     tile = vals_v.shape[2]
     slots = vals_v.shape[1]
     per_dev = rows // tile
@@ -140,7 +136,7 @@
                     ring_copy(buf, which, hop, own, k).start()
                 sib_copy(part(buf, hop, own, k), which, sib.at[which, hop - 1, 0 if own else 1]).start()
                 return 0
-            lax.fori_loop(0, CHUNKS, one, 0)
+            lax.fori_loop(0, CHUNKS, one, 0, unroll=True)
 
     def sib_in(buf, which, hop):
         for i in range(2 if hop < half else 1):
@@ -191,8 +187,8 @@
         for j in range(width // tile):
             inv[pl.ds(i * tile, tile), pl.ds(j * tile, tile)] = square
 
-    left[0] = feats_all[row]
-    base[...] = matmul(left[0], ws_v[...])
+    left[0] = jnp.transpose(feats_all[row])
+    base[...] = matmul(feats_all[row], ws_v[...])
     acc[...] = jnp.zeros_like(acc)
     add(feats_all, 0)
     for hop in range(1, half + 1):
@@ -213,9 +209,9 @@
         if i + 1 < rounds:
             relay_send(i + 1)
 
-    left[1] = (acc[...] * inv[...]).astype(BF16)
-    base[...] += matmul(left[1], wn_v[...])
-    pre = base[...]
+    aggregate = (acc[...] * inv[...]).astype(BF16)
+    pre = base[...] + matmul(aggregate, wn_v[...])
+    left[1] = jnp.transpose(aggregate)
     sig = jax.nn.sigmoid(pre)
     gp[...] = (cot_v[...].astype(F32) * sig * (1.0 + pre * (1.0 - sig))).astype(BF16)
     def far_first(count):
@@ -251,11 +247,11 @@
     write_wg = pltpu.make_async_copy(r5, wgrad.at[core], out_sem.at[2])
 
     def stage0():
-        pair_out[...] = matmul_tn(left[other], gp[...]).astype(BF16)
+        pair_out[...] = matmul(left[other], gp[...]).astype(BF16)
         pair.start()
         hidden_all[row] = (matmul_nt(gp[...], wn_v[...]) * inv[...]).astype(BF16)
         launch_own(hidden_all, 1, hidden_all.at[row])
-        keep[...] = matmul_tn(left[core], gp[...])
+        keep[...] = matmul(left[core], gp[...])
 
     def stage1():
         pair.wait_recv()
@@ -339,10 +335,23 @@
     write_wg.wait()
 
 
-def deliver(out_in, fgrad_in, wgrad_in, out, fgrad, wgrad):
-    out[...] = out_in[...]
-    fgrad[...] = fgrad_in[...]
-    wgrad[...] = wgrad_in[...].astype(F32).reshape(wgrad.shape)
+def deliver(out_in, fgrad_in, wgrad_in, out, fgrad, wgrad, out_v, fgrad_v, narrow, wide, sem_in, sem_out):
+    halves = wgrad.shape[0]
+    loads = [pltpu.make_async_copy(wgrad_in.at[i], narrow.at[i], sem_in.at[i]) for i in range(halves)]
+    loads.append(pltpu.make_async_copy(out_in, out_v, sem_in.at[halves]))
+    loads.append(pltpu.make_async_copy(fgrad_in, fgrad_v, sem_in.at[halves + 1]))
+    stores = [pltpu.make_async_copy(wide.at[i], wgrad.at[i], sem_out.at[i]) for i in range(halves)]
+    stores.append(pltpu.make_async_copy(out_v, out, sem_out.at[halves]))
+    stores.append(pltpu.make_async_copy(fgrad_v, fgrad, sem_out.at[halves + 1]))
+    for load in loads:
+        load.start()
+    for i in range(halves + 2):
+        loads[i].wait()
+        if i < halves:
+            wide[i] = narrow[i].astype(F32).reshape(wide.shape[1:])
+        stores[i].start()
+    for store in stores:
+        store.wait()
 
 
 def solution(mesh):
@@ -386,7 +395,7 @@
                 pltpu.VMEM(block, F32),
                 pltpu.VMEM(block, F32),
                 pltpu.VMEM(block, F32),
-                pltpu.VMEM((2,) + block, BF16),
+                pltpu.VMEM((2, width, rows), BF16),
                 pltpu.VMEM(block, BF16),
                 pltpu.VMEM(block, BF16),
                 pltpu.VMEM(block, BF16),
@@ -412,7 +421,6 @@
                 collective_id=0, has_side_effects=True, vmem_limit_bytes=56 * 1024 * 1024),
         )(
             tile_cols, features, cotangent, degrees.reshape(row_tiles, tile), tile_vals, w_self, w_neigh)
-        whole = pl.BlockSpec(memory_space=pltpu.VMEM)
         return pl.pallas_call(
             deliver,
             out_shape=(
@@ -420,8 +428,16 @@
                 jax.ShapeDtypeStruct(block, BF16),
                 jax.ShapeDtypeStruct((2, width, width), F32),
             ),
-            in_specs=[whole] * 3,
-            out_specs=(whole,) * 3,
+            in_specs=[any_spec] * 3,
+            out_specs=(any_spec,) * 3,
+            scratch_shapes=[
+                pltpu.VMEM(block, BF16),
+                pltpu.VMEM(block, BF16),
+                pltpu.VMEM((2, side, piece, width), BF16),
+                pltpu.VMEM((2, width, width), F32),
+                dma((4,)),
+                dma((4,)),
+            ],
             compiler_params=pltpu.CompilerParams(vmem_limit_bytes=56 * 1024 * 1024),
         )(*results)
 

time: 63.1 us -> 63 us (level)
  no operation moved by 1% of the time
where the time goes in v4:
time: 63 us; the launch traced here: 62.8 us
  Pallas kernels  62.2 us (99%)
  between operations  0.64 us (1%)
    pallas_call x1, Pallas kernels, shards(): pl.pallas_call(functools.partial(layer_kernel, side, depth, scale), out_s...  60.3 us
    pallas_call x1, Pallas kernels, shards(): pl.pallas_call(deliver, out_shape=(jax.ShapeDtypeStruct(block, BF16), jax...  1.86 us

profile of v4, /device:TPU:1, one launch (start us, length us, event | category | flops | bytes accessed | tf_op | source)
XLA Modules:
  0.0 62.8 jit_solution(1140398369766662807)
XLA Ops:
  0.6 60.3 %shard_map.94 = (bf16[256,256]{1,0:T(8,128)(2,1)}, bf16[256,256]{1,0:T(8,128)(2,1)}, bf16[2,8,32,256]{3,2,1,0:T(8,128)(2,1)}) custom-call(s32[2,17]{1,0:T(2,128)} %cols_in.1, bf16[256,256]{1,0:T(8,128)(2,1)} %feat.1, bf16[256,256]{1,0:T(8,128)(2,1)} %cot.1, s32[2,128]{1,0:T(2,128)} %bitcast.1, bf16[2,17,128,128]{3,2,1,0:T(8,128)(2,1)} %vals.1, ...), custom_call_target="tpu_custom_call" | custom-call | tf_op jit(solution)/shard_map/pallas_call | solution.py:374
  61.0 1.9 %shard_map.95 = (bf16[256,256]{1,0:T(8,128)(2,1)}, bf16[256,256]{1,0:T(8,128)(2,1)}, f32[2,256,256]{2,1,0:T(8,128)}) custom-call(bf16[256,256]{1,0:T(8,128)(2,1)} %get-tuple-element.6.out_in, bf16[256,256]{1,0:T(8,128)(2,1)} %get-tuple-element.7.fgrad_in, bf16[2,8,32,256]{3,2,1,0:T(8,128)(2,1)} %get-tuple-element.8.wgrad_in), custom_call_target="tpu_custom_call" | custom-call | tf_op jit(solution)/shard_map/pallas_call | solution.py:424
